TPU v7x, 256 devices: a whole 4x4x8 slice. The times are simulated.
256 devices in a mesh: space: 64 (over x, y_lo, z), modes: 4 (over y_hi, core).
Axes of the slice: x: 4, y: 4 (y_hi: 2, y_lo: 2; y = y_hi * 2 + y_lo), z: 8, core: 2. Of those that a mesh axis runs over, the one named last changes fastest.
Arguments:
- pressure: float32 [256, 1024, 512], P('modes', 'space'), may hold values from -6 to 6
- gap_terms: float32 [8, 1024, 512], P(None, 'space'), may hold values from 0.05 to 0.5
- coupling: float32 [8, 256, 256], replicated, may hold values from -0.1875 to 0.1875
- pattern: int32 [8, 4, 4], replicated, may hold values 0 or 1
Outputs:
- damped: float32 [256, 1024, 512], P('modes', 'space')
All inputs are finite; a program needn't handle non-finite values.
Results may differ from a plain program's by a relative error of at most 0.0001.
Values sent between devices are 32-bit elements; how exact they have to be, the bound alone decides.
A program may use at most 128 MiB of HBM per device.

v0:
```python
import jax
import jax.numpy as jnp
from jax import lax
from jax.experimental import pallas as pl
from jax.experimental.pallas import tpu as pltpu
from jax.sharding import PartitionSpec as P

MESH = pl.DeviceIdType.MESH
K = 8
MODES = 256
BLOCK = 64
ROWS = 16
LANES = 128
ZRUN = 8
GROUPS = MODES // 16
CHUNKS = 6
F32 = jnp.float32
BF16 = jnp.bfloat16


def lane_iota(rows):
    return lax.broadcasted_iota(jnp.int32, (rows, LANES), 1)


def split(value):
    high = value.astype(BF16)
    return high, (value - high.astype(F32)).astype(BF16)


def kernel(
    press, gap, coupling, pattern, out,
    strip, gap_in, coup, rows_v, first, extra, extra1, extra_own, damp, home, sendrows,
    gap_pad, c_right, c_left, c_down, e_coef, mix_hi, mix_lo, x_hi, x_lo, halo_out, halo_in,
    load_sem, in_send, in_recv, z_send, z_recv, out_send, out_recv, store_sem,
):
    space = lax.axis_index("space")
    mode = lax.axis_index("modes")
    count = lax.axis_size("space")
    y_lo = lax.rem(lax.div(space, ZRUN), 2)

    def swapped(index, bit):
        return index + bit * (lax.rem(index, 2) * 2 + lax.div(index, 2) - index)

    quarter = swapped(mode, y_lo)
    hi, core = lax.div(mode, 2), lax.rem(mode, 2)
    group = [(1 - hi) * 2 + core, (1 - hi) * 2 + 1 - core, hi * 2 + 1 - core]
    group_quarter = [swapped(peer, y_lo) for peer in group]

    def beside(step):
        other = lax.rem(space + step + count, count)
        other_y = lax.rem(lax.div(other, ZRUN), 2)
        return (other, swapped(quarter, other_y))

    before, after = beside(-1), beside(1)

    def columns(t):
        return slice(t * LANES, (t + 1) * LANES)

    press_loads = [pltpu.make_async_copy(press.at[:, columns(t)], strip.at[t], load_sem.at[t]) for t in range(4)]
    gap_loads = [pltpu.make_async_copy(gap.at[:, columns(t)], gap_in.at[t], load_sem.at[4 + t]) for t in range(4)]
    coup_load = pltpu.make_async_copy(coupling, coup, load_sem.at[8])
    for load in press_loads + gap_loads + [coup_load]:
        load.start()

    barrier = pltpu.get_barrier_semaphore()
    for peer in group:
        pl.semaphore_signal(barrier, inc=1, device_id=(space, peer), device_id_type=MESH)
    for peer in (before, after):
        pl.semaphore_signal(barrier, inc=1, device_id=peer, device_id_type=MESH)

    for load in gap_loads:
        load.wait()
    for r in range(ROWS):
        slabs = [gap_in[t, pl.ds(r, K, stride=ROWS), :] for t in range(4)]
        slabs = [jnp.broadcast_to(slabs[0][:, :1], (K, LANES)), *slabs, jnp.broadcast_to(slabs[3][:, LANES - 1 :], (K, LANES))]
        for t in range(6):
            gap_pad[r + 2, :, columns(t)] = slabs[t]

    for load in press_loads:
        load.wait()

    def own_rows(r):
        for t in range(4):
            sendrows[t, r] = strip[t, pl.ds(r, BLOCK, stride=ROWS), :]

    for r in (0, 1, 14, 15):
        own_rows(r)

    pl.semaphore_wait(barrier, 5)

    mine = pl.multiple_of(mode * BLOCK, BLOCK)

    def row_copy(peer, peer_quarter, row, rows, slot, source):
        return pltpu.make_async_remote_copy(
            src_ref=sendrows.at[peer_quarter, pl.ds(row, rows)],
            dst_ref=rows_v.at[pl.ds(row + 2, rows), pl.ds(pl.multiple_of(source * BLOCK, BLOCK), BLOCK)],
            send_sem=in_send.at[slot, peer],
            recv_sem=in_recv.at[slot, source],
            device_id=(space, peer),
            device_id_type=MESH,
        )

    def extra_copy(peer, peer_quarter, source):
        return pltpu.make_async_remote_copy(
            src_ref=extra_own.at[peer_quarter],
            dst_ref=extra.at[pl.ds(pl.multiple_of(source * BLOCK, BLOCK), BLOCK)],
            send_sem=in_send.at[CHUNKS + 2, peer],
            recv_sem=in_recv.at[CHUNKS + 2, source],
            device_id=(space, peer),
            device_id_type=MESH,
        )

    for row, slot in ((0, CHUNKS), (14, CHUNKS + 1)):
        for peer, peer_quarter in zip(group, group_quarter):
            row_copy(peer, peer_quarter, row, 2, slot, mode).start()

    def z_copy(source, target, slot, device):
        return pltpu.make_async_remote_copy(
            src_ref=source, dst_ref=target, send_sem=z_send.at[slot], recv_sem=z_recv.at[slot],
            device_id=device, device_id_type=MESH,
        )

    gap_copies = [
        z_copy(gap_pad.at[pl.ds(2, 2)], gap_pad.at[pl.ds(ROWS + 2, 2)], 0, before),
        z_copy(gap_pad.at[pl.ds(ROWS, 2)], gap_pad.at[pl.ds(0, 2)], 1, after),
    ]
    for copy in gap_copies:
        copy.start()

    for r in range(2, 14):
        own_rows(r)

    def own_extra(g, carry):
        at = pl.ds(pl.multiple_of(g * 8, 8), 8)
        lane = lane_iota(8)
        built = [jnp.zeros((8, LANES), F32) for _ in range(4)]
        for r in range(ROWS):
            rolled = [pltpu.roll(sendrows[t, r, at, :], 2, 1) for t in range(4)]
            edges = [jnp.where(lane < 2, 0.0, rolled[0])]
            edges += [jnp.where(lane < 2, rolled[b - 1], rolled[b]) for b in range(1, 4)]
            edges.append(jnp.where(lane < 2, rolled[3], 0.0))
            start = 6 * (r + 2)
            for t in range(4):
                both = jnp.where(lane < 3, edges[t], pltpu.roll(edges[t + 1], 2, 1))
                inside = (lane >= start) & (lane < start + 6)
                built[t] = jnp.where(inside, pltpu.roll(both, start, 1), built[t])
        for t in range(4):
            extra_own[t, at, :] = built[t]
        return carry

    lax.fori_loop(0, BLOCK // 8, own_extra, 0)
    for peer, peer_quarter in zip(group, group_quarter):
        extra_copy(peer, peer_quarter, mode).start()

    for c in range(CHUNKS):
        for peer, peer_quarter in zip(group, group_quarter):
            row_copy(peer, peer_quarter, 2 * c + 2, 2, c, mode).start()

    extra[pl.ds(mine, BLOCK), :] = extra_own[quarter]
    for r in range(ROWS):
        rows_v[r + 2, pl.ds(mine, BLOCK), :] = sendrows[quarter, r]

    coup_load.wait()
    wide = lax.broadcasted_iota(jnp.int32, (BLOCK, MODES), 1)
    for k in range(K):
        for b in range(4):
            scale = [pattern[k, b, c].astype(F32) for c in range(4)]
            factor = jnp.where(
                wide < 128,
                jnp.where(wide < 64, scale[0], scale[1]),
                jnp.where(wide < 192, scale[2], scale[3]),
            )
            high, low = split(coup[k, b * BLOCK : (b + 1) * BLOCK, :] * factor)
            mix_hi[b * BLOCK : (b + 1) * BLOCK, k * MODES : (k + 1) * MODES] = high
            mix_lo[b * BLOCK : (b + 1) * BLOCK, k * MODES : (k + 1) * MODES] = low

    for copy in gap_copies:
        copy.wait_recv()

    @pl.when(space == 0)
    def _():
        gap_pad[1] = gap_pad[2]

    @pl.when(space == count - 1)
    def _():
        gap_pad[ROWS + 2] = gap_pad[ROWS + 1]

    def tile(index, side):
        return gap_pad[index, :, pl.ds(pl.multiple_of((quarter + side) * LANES, LANES), LANES)]

    lane8 = lane_iota(8)

    def coefficients(index, slab):
        left, here, right = tile(index, 0), tile(index, 1), tile(index, 2)
        below = tile(jnp.minimum(index + 1, ROWS + 3), 1)
        next_cell = jnp.where(lane8 == LANES - 1, pltpu.roll(right, LANES - 1, 1), pltpu.roll(here, LANES - 1, 1))
        last_cell = jnp.where(lane8 == 0, pltpu.roll(left, 1, 1), pltpu.roll(here, 1, 1))
        for ref, value in ((c_right, next_cell), (c_left, last_cell), (c_down, below)):
            face = 0.5 * (here + value)
            for k in range(K):
                ref[index, k] = jnp.broadcast_to(face[k : k + 1, :], (8, LANES))
        edge_left = jnp.where(lane8 < 2, pltpu.roll(left, 2, 1), pltpu.roll(here, 2, 1))
        edge_right = jnp.where(lane8 < 2, pltpu.roll(here, 2, 1), pltpu.roll(right, 2, 1))
        both = jnp.where(lane8 < 3, edge_left, pltpu.roll(edge_right, 2, 1))
        start = 6 * index
        return jnp.where((lane8 >= start) & (lane8 < start + 6), pltpu.roll(both, start, 1), slab)

    slab = lax.fori_loop(0, ROWS + 4, coefficients, jnp.zeros((8, LANES), F32))
    for n, shift in enumerate((LANES - 1, 1, LANES - 6, 6)):
        face = 0.5 * (slab + pltpu.roll(slab, shift, 1))
        for k in range(K):
            e_coef[n, k] = jnp.broadcast_to(face[k : k + 1, :], (8, LANES))

    for slot, row in ((CHUNKS, 0), (CHUNKS + 1, 14)):
        for peer in group:
            row_copy(peer, 0, row, 2, slot, peer).wait_recv()
    for peer in group:
        extra_copy(peer, 0, peer).wait_recv()

    lane32 = lane_iota(32)
    for n, shift in enumerate((LANES - 12, 32)):
        packed = jnp.zeros((32, LANES), F32)
        for g in range(8):
            moved = pltpu.roll(extra[32 * g : 32 * g + 32, :], (shift + 16 * g) % LANES, 1)
            packed = jnp.where((lane32 >= 16 * g) & (lane32 < 16 * g + 16), moved, packed)
        halo_out[n] = packed

    edge_copies = [
        z_copy(halo_out.at[0], halo_in.at[1], 2, before),
        z_copy(halo_out.at[1], halo_in.at[0], 3, after),
        z_copy(rows_v.at[pl.ds(2, 2)], rows_v.at[pl.ds(ROWS + 2, 2)], 4, before),
        z_copy(rows_v.at[pl.ds(ROWS, 2)], rows_v.at[pl.ds(0, 2)], 5, after),
    ]
    for copy in edge_copies:
        copy.start()
    for copy in edge_copies:
        copy.wait_recv()

    top, bottom = space == 0, space == count - 1

    @pl.when(top)
    def _():
        rows_v[0:2] = jnp.zeros((2, MODES, LANES), F32)

    @pl.when(bottom)
    def _():
        rows_v[ROWS + 2 :] = jnp.zeros((2, MODES, LANES), F32)

    upper = jnp.where(top, 0.0, halo_in[0])
    lower = jnp.where(bottom, 0.0, halo_in[1])
    for g in range(8):
        at = slice(32 * g, 32 * g + 32)
        value = jnp.where(lane32 < 12, pltpu.roll(upper, (LANES - 16 * g) % LANES, 1), extra[at, :])
        inside = (lane32 >= 108) & (lane32 < 120)
        extra[at, :] = jnp.where(inside, pltpu.roll(lower, (108 - 16 * g) % LANES, 1), value)

    def twice(value):
        return jnp.concatenate([value, value], axis=0)

    def put(k, g, column, value):
        high, low = split(value)
        at = pl.ds(pl.multiple_of(k * MODES + g * 16, 16), 16)
        x_hi[at, column : column + LANES] = high
        x_lo[at, column : column + LANES] = low

    def product(width):
        return (
            jnp.dot(mix_hi[...], x_hi[:, :width], preferred_element_type=F32)
            + jnp.dot(mix_hi[...], x_lo[:, :width], preferred_element_type=F32)
            + jnp.dot(mix_lo[...], x_hi[:, :width], preferred_element_type=F32)
        )

    def extra_terms(g, carry):
        v = extra[pl.ds(pl.multiple_of(g * 16, 16), 16), :]
        diffs = [v - pltpu.roll(v, shift, 1) for shift in (LANES - 1, 1, LANES - 6, 6)]
        for k in range(K):
            total = twice(e_coef[0, k]) * diffs[0]
            for n in range(1, 4):
                total = total + twice(e_coef[n, k]) * diffs[n]
            put(k, g, 0, total)
        return carry

    lax.fori_loop(0, GROUPS, extra_terms, 0)
    column = lax.rem(lane_iota(MODES), 6)
    outside = ((column == 1) & (quarter == 0)) | ((column == 4) & (quarter == 3))
    extra1[...] = jnp.where(outside, 0.0, product(LANES))

    lane16 = lane_iota(16)

    def terms(source, base, sides, index):
        def body(g, carry):
            at = pl.ds(pl.multiple_of(g * 16, 16), 16)
            v = [source[base + n, at, :] for n in range(4)]
            side = sides[at, :]
            down = [v[n] - v[n + 1] for n in range(3)]
            diffs = []
            for n in range(2):
                here = v[n + 1]
                lane = 6 * (index + n)
                left = jnp.where(lane16 == 0, pltpu.roll(side, LANES - 1 - lane, 1), pltpu.roll(here, 1, 1))
                right = jnp.where(
                    lane16 == LANES - 1, pltpu.roll(side, LANES - 5 - lane, 1), pltpu.roll(here, LANES - 1, 1)
                )
                diffs.append((here - left, here - right))
            for k in range(K):
                flux = [twice(c_down[index - 1 + n, k]) * down[n] for n in range(3)]
                for n in range(2):
                    total = twice(c_left[index + n, k]) * diffs[n][0] + twice(c_right[index + n, k]) * diffs[n][1]
                    put(k, g, n * LANES, total + (flux[n + 1] - flux[n]))
            return carry

        lax.fori_loop(0, GROUPS, body, 0)

    def home_copy(peer, owner_of_block, pair, their_quarter):
        return pltpu.make_async_remote_copy(
            src_ref=damp.at[pl.ds(2 * pair, 2), pl.ds(pl.multiple_of(owner_of_block * BLOCK, BLOCK), BLOCK)],
            dst_ref=home.at[their_quarter, pl.ds(2 * pair, 2)],
            send_sem=out_send.at[pair, peer],
            recv_sem=out_recv.at[pair, their_quarter],
            device_id=(space, peer),
            device_id_type=MESH,
        )

    def step(i, carry):
        @pl.when((i >= 1) & (i <= CHUNKS))
        def _():
            for peer in group:
                row_copy(peer, 0, 2 * i, 2, i - 1, peer).wait_recv()

        terms(rows_v, 2 * i, extra, 2 * i + 1)
        result = product(2 * LANES)
        first[2 * i] = jnp.where(top & (i == 0), 0.0, result[:, :LANES])
        first[2 * i + 1] = jnp.where(bottom & (i == ROWS // 2), 0.0, result[:, LANES:])

        @pl.when(i >= 1)
        def _():
            j = i - 1
            terms(first, 2 * j, extra1, 2 * j + 2)
            result = product(2 * LANES)
            damp[2 * j] = result[:, :LANES]
            damp[2 * j + 1] = result[:, LANES:]
            for peer in group:
                home_copy(peer, peer, j, quarter).start()

        return carry

    lax.fori_loop(0, ROWS // 2 + 1, step, 0)

    for pair in range(ROWS // 2):
        for peer, peer_quarter in zip(group, group_quarter):
            home_copy(peer, mode, pair, peer_quarter).wait_recv()
        for r in (2 * pair, 2 * pair + 1):
            home[quarter, r] = damp[r, pl.ds(mine, BLOCK), :]
            for t in range(4):
                strip[t, pl.ds(r, BLOCK, stride=ROWS), :] = home[t, r]
    stores = [pltpu.make_async_copy(strip.at[t], out.at[:, columns(t)], store_sem.at[t]) for t in range(4)]
    for store in stores:
        store.start()

    for slot, row in [(c, 2 * c + 2) for c in range(CHUNKS)] + [(CHUNKS, 0), (CHUNKS + 1, 14)]:
        for peer in group:
            row_copy(peer, 0, row, 2, slot, mode).wait_send()
    for peer in group:
        extra_copy(peer, 0, mode).wait_send()
        for pair in range(ROWS // 2):
            home_copy(peer, peer, pair, quarter).wait_send()
    for copy in gap_copies + edge_copies:
        copy.wait_send()
    for store in stores:
        store.wait()


def per_device(pressure, gap_terms, coupling, pattern):
    cells = pressure.shape[2]
    vmem = pltpu.VMEM
    result = pl.pallas_call(
        kernel,
        out_shape=jax.ShapeDtypeStruct((BLOCK * ROWS, cells), F32),
        in_specs=[
            pl.BlockSpec(memory_space=pl.ANY),
            pl.BlockSpec(memory_space=pl.ANY),
            pl.BlockSpec(memory_space=pl.ANY),
            pl.BlockSpec(memory_space=pltpu.SMEM),
        ],
        out_specs=pl.BlockSpec(memory_space=pl.ANY),
        scratch_shapes=[
            vmem((4, BLOCK * ROWS, LANES), F32),
            vmem((4, K * ROWS, LANES), F32),
            vmem((K, MODES, MODES), F32),
            vmem((ROWS + 4, MODES, LANES), F32),
            vmem((ROWS + 2, MODES, LANES), F32),
            vmem((MODES, LANES), F32),
            vmem((MODES, LANES), F32),
            vmem((4, BLOCK, LANES), F32),
            vmem((ROWS, MODES, LANES), F32),
            vmem((4, ROWS, BLOCK, LANES), F32),
            vmem((4, ROWS, BLOCK, LANES), F32),
            vmem((ROWS + 4, K, cells + 2 * LANES), F32),
            vmem((ROWS + 4, K, 8, LANES), F32),
            vmem((ROWS + 4, K, 8, LANES), F32),
            vmem((ROWS + 4, K, 8, LANES), F32),
            vmem((4, K, 8, LANES), F32),
            vmem((MODES, K * MODES), BF16),
            vmem((MODES, K * MODES), BF16),
            vmem((K * MODES, 2 * LANES), BF16),
            vmem((K * MODES, 2 * LANES), BF16),
            vmem((2, 32, LANES), F32),
            vmem((2, 32, LANES), F32),
            pltpu.SemaphoreType.DMA((9,)),
            pltpu.SemaphoreType.DMA((CHUNKS + 3, 4)),
            pltpu.SemaphoreType.DMA((CHUNKS + 3, 4)),
            pltpu.SemaphoreType.DMA((6,)),
            pltpu.SemaphoreType.DMA((6,)),
            pltpu.SemaphoreType.DMA((ROWS // 2, 4)),
            pltpu.SemaphoreType.DMA((ROWS // 2, 4)),
            pltpu.SemaphoreType.DMA((4,)),
        ],
        compiler_params=pltpu.CompilerParams(
            collective_id=0, has_side_effects=True, vmem_limit_bytes=56 * 1024 * 1024
        ),
        cost_estimate=pl.CostEstimate(flops=26_000_000_000, bytes_accessed=7_000_000, transcendentals=0),
        name="galerkin_twice",
    )(pressure.reshape(BLOCK * ROWS, cells), gap_terms.reshape(K * ROWS, cells), coupling, pattern)
    return result.reshape(pressure.shape)


def solution(mesh):
    placed = (P("modes", "space", None), P(None, "space", None), P(), P())
    return jax.shard_map(
        per_device, mesh=mesh, in_specs=placed, out_specs=P("modes", "space", None), check_vma=False
    )
```

profile of v0, /device:TPU:1, one launch (start us, length us, event | category | flops | bytes accessed | tf_op | source)
XLA Modules:
  0.0 98.4 jit_solution(9388955875608766971)
XLA Ops:
  0.0 1.4 %copy.5.pattern = s32[8,4,4]{2,1,0:T(4,128)} copy(s32[8,4,4]{0,2,1:T(4,128)} %param.7) | data formatting | bytes 1024 | tf_op args[3]
  1.4 93.8 %galerkin_twice.1 = f32[1024,512]{1,0:T(8,128)} custom-call(f32[1024,512]{1,0:T(8,128)} %bitcast.4, f32[128,512]{1,0:T(8,128)} %bitcast.5, f32[8,256,256]{2,1,0:T(8,128)} %coupling.1, s32[8,4,4]{2,1,0:T(4,128)} %copy.5.pattern), custom_call_target="tpu_custom_call" | custom-call | flops 25999998976 | bytes 7000000 | tf_op jit(solution)/shard_map/galerkin_twice/pallas_call | solution.py:376
  95.2 3.2 %copy.7 = f32[64,16,512]{2,1,0:T(8,128)} copy(f32[64,16,512]{2,1,0:T(8,128)} %bitcast.3) | data formatting | bytes 4194304
where the time goes:
time: 98.7 us; the launch traced here: 98.4 us
  Pallas kernels  93.8 us (95%)
  local copies, waits for them, and re-layouts  4.61 us (5%)
    pallas_call x1, Pallas kernels, per_device(): pl.pallas_call(kernel, out_shape=jax.ShapeDtypeStruct((BLOCK * ROWS, cell...  93.8 us
    unnamed x2, local copies, waits for them, and re-layouts  4.61 us

commit v1 on v0

v1 whole, which is shorter than its diff:
```python
import jax
import jax.numpy as jnp
from jax import lax
from jax.experimental import pallas as pl
from jax.experimental.pallas import tpu as pltpu
from jax.sharding import PartitionSpec as P

MESH = pl.DeviceIdType.MESH
K = 8
MODES = 256
BLOCK = 64
ROWS = 16
LANES = 128
ZRUN = 8
GROUPS = MODES // 16
CHUNKS = 6
FIRST = ROWS + 4
DAMPED = 2 * ROWS + 6
F32 = jnp.float32
BF16 = jnp.bfloat16


def lane_iota(rows):
    return lax.broadcasted_iota(jnp.int32, (rows, LANES), 1)


def split(value):
    high = value.astype(BF16)
    return high, (value - high.astype(F32)).astype(BF16)


def kernel(
    press, gap, coupling, pattern, home,
    strip, gap_in, coup, pattern_in, rows_v, extra, extra_own, sendrows,
    gap_pad, c_right, c_left, c_down, e_coef, mix_hi, mix_lo, x_hi, x_lo, halo_out, halo_in,
    load_sem, in_send, in_recv, z_send, z_recv, out_send, out_recv, own_sem,
):
    space = lax.axis_index("space")
    mode = lax.axis_index("modes")
    count = lax.axis_size("space")
    y_lo = lax.rem(lax.div(space, ZRUN), 2)

    def swapped(index, bit):
        return index + bit * (lax.rem(index, 2) * 2 + lax.div(index, 2) - index)

    quarter = swapped(mode, y_lo)
    hi, core = lax.div(mode, 2), lax.rem(mode, 2)
    group = [(1 - hi) * 2 + core, (1 - hi) * 2 + 1 - core, hi * 2 + 1 - core]
    group_quarter = [swapped(peer, y_lo) for peer in group]

    def beside(step):
        other = lax.rem(space + step + count, count)
        other_y = lax.rem(lax.div(other, ZRUN), 2)
        return (other, swapped(quarter, other_y))

    before, after = beside(-1), beside(1)

    def columns(t):
        return slice(t * LANES, (t + 1) * LANES)

    press_loads = [pltpu.make_async_copy(press.at[:, columns(t)], strip.at[t], load_sem.at[t]) for t in range(4)]
    gap_loads = [pltpu.make_async_copy(gap.at[:, columns(t)], gap_in.at[t], load_sem.at[4 + t]) for t in range(4)]
    coup_load = pltpu.make_async_copy(coupling, coup, load_sem.at[8])
    pattern_load = pltpu.make_async_copy(pattern, pattern_in, load_sem.at[9])
    for load in press_loads + gap_loads + [coup_load, pattern_load]:
        load.start()

    barrier = pltpu.get_barrier_semaphore()
    for peer in group:
        pl.semaphore_signal(barrier, inc=1, device_id=(space, peer), device_id_type=MESH)
    for peer in (before, after):
        pl.semaphore_signal(barrier, inc=1, device_id=peer, device_id_type=MESH)

    for load in press_loads:
        load.wait()

    def own_rows(g, carry):
        at = pl.ds(pl.multiple_of(g * 8, 8), 8)
        lane = lane_iota(8)
        parts = [jnp.zeros((8, LANES), F32) for _ in range(4)]
        for r in range(ROWS):
            start = 6 * (r + 2)
            inside = (lane >= start) & (lane < start + 4)
            for t in range(4):
                value = strip[t, pl.ds(g * (8 * ROWS) + r, 8, stride=ROWS), :]
                sendrows[t, r, at, :] = value
                parts[t] = jnp.where(inside, pltpu.roll(value, start + 2, 1), parts[t])
        nothing = jnp.zeros((8, LANES), F32)
        place = lax.rem(lane, 6)
        moved = [pltpu.roll(part, 2, 1) for part in parts] + [nothing]
        for t in range(4):
            left = parts[t - 1] if t else nothing
            value = jnp.where(place < 2, left, jnp.where(place == 2, parts[t], moved[t]))
            extra_own[t, at, :] = jnp.where(place < 4, value, moved[t + 1])
        return carry

    lax.fori_loop(0, BLOCK // 8, own_rows, 0)

    pl.semaphore_wait(barrier, 5)

    mine = pl.multiple_of(mode * BLOCK, BLOCK)

    def row_copy(peer, peer_quarter, row, rows, slot, source):
        return pltpu.make_async_remote_copy(
            src_ref=sendrows.at[peer_quarter, pl.ds(row, rows)],
            dst_ref=rows_v.at[pl.ds(row + 2, rows), pl.ds(pl.multiple_of(source * BLOCK, BLOCK), BLOCK)],
            send_sem=in_send.at[slot, peer],
            recv_sem=in_recv.at[slot, source],
            device_id=(space, peer),
            device_id_type=MESH,
        )

    def extra_copy(peer, peer_quarter, source):
        return pltpu.make_async_remote_copy(
            src_ref=extra_own.at[peer_quarter],
            dst_ref=extra.at[0, pl.ds(pl.multiple_of(source * BLOCK, BLOCK), BLOCK)],
            send_sem=in_send.at[CHUNKS + 2, peer],
            recv_sem=in_recv.at[CHUNKS + 2, source],
            device_id=(space, peer),
            device_id_type=MESH,
        )

    for row, slot in ((0, CHUNKS), (14, CHUNKS + 1)):
        for peer, peer_quarter in zip(group, group_quarter):
            row_copy(peer, peer_quarter, row, 2, slot, mode).start()
    for peer, peer_quarter in zip(group, group_quarter):
        extra_copy(peer, peer_quarter, mode).start()
    for c in range(CHUNKS):
        for peer, peer_quarter in zip(group, group_quarter):
            row_copy(peer, peer_quarter, 2 * c + 2, 2, c, mode).start()

    for load in gap_loads:
        load.wait()
    for r in range(ROWS):
        slabs = [gap_in[t, pl.ds(r, K, stride=ROWS), :] for t in range(4)]
        slabs = [jnp.broadcast_to(slabs[0][:, :1], (K, LANES)), *slabs, jnp.broadcast_to(slabs[3][:, LANES - 1 :], (K, LANES))]
        for t in range(6):
            gap_pad[r + 2, :, columns(t)] = slabs[t]

    def z_copy(source, target, slot, device):
        return pltpu.make_async_remote_copy(
            src_ref=source, dst_ref=target, send_sem=z_send.at[slot], recv_sem=z_recv.at[slot],
            device_id=device, device_id_type=MESH,
        )

    gap_copies = [
        z_copy(gap_pad.at[pl.ds(2, 2)], gap_pad.at[pl.ds(ROWS + 2, 2)], 0, before),
        z_copy(gap_pad.at[pl.ds(ROWS, 2)], gap_pad.at[pl.ds(0, 2)], 1, after),
    ]
    for copy in gap_copies:
        copy.start()

    extra[0, pl.ds(mine, BLOCK), :] = extra_own[quarter]
    for r in range(ROWS):
        rows_v[r + 2, pl.ds(mine, BLOCK), :] = sendrows[quarter, r]

    coup_load.wait()
    pattern_load.wait()
    wide = lax.broadcasted_iota(jnp.int32, (1, MODES), 1)
    for k in range(K):
        for b in range(4):
            scale = [pattern_in[b, c : c + 1, k : k + 1].astype(F32) for c in range(4)]
            factor = jnp.where(
                wide < 128,
                jnp.where(wide < 64, scale[0], scale[1]),
                jnp.where(wide < 192, scale[2], scale[3]),
            )
            high, low = split(coup[k, b * BLOCK : (b + 1) * BLOCK, :] * factor)
            mix_hi[b * BLOCK : (b + 1) * BLOCK, k * MODES : (k + 1) * MODES] = high
            mix_lo[b * BLOCK : (b + 1) * BLOCK, k * MODES : (k + 1) * MODES] = low

    for copy in gap_copies:
        copy.wait_recv()

    @pl.when(space == 0)
    def _():
        gap_pad[1] = gap_pad[2]

    @pl.when(space == count - 1)
    def _():
        gap_pad[ROWS + 2] = gap_pad[ROWS + 1]

    def tile(index, side):
        return gap_pad[index, :, pl.ds(pl.multiple_of((quarter + side) * LANES, LANES), LANES)]

    lane8 = lane_iota(8)

    def coefficients(index, slab):
        left, here, right = tile(index, 0), tile(index, 1), tile(index, 2)
        below = tile(jnp.minimum(index + 1, ROWS + 3), 1)
        next_cell = jnp.where(lane8 == LANES - 1, pltpu.roll(right, LANES - 1, 1), pltpu.roll(here, LANES - 1, 1))
        last_cell = jnp.where(lane8 == 0, pltpu.roll(left, 1, 1), pltpu.roll(here, 1, 1))
        for ref, value in ((c_right, next_cell), (c_left, last_cell), (c_down, below)):
            ref[index] = 0.5 * (here + value)
        edge_left = jnp.where(lane8 < 2, pltpu.roll(left, 2, 1), pltpu.roll(here, 2, 1))
        edge_right = jnp.where(lane8 < 2, pltpu.roll(here, 2, 1), pltpu.roll(right, 2, 1))
        both = jnp.where(lane8 < 3, edge_left, pltpu.roll(edge_right, 2, 1))
        start = 6 * index
        return jnp.where((lane8 >= start) & (lane8 < start + 6), pltpu.roll(both, start, 1), slab)

    slab = lax.fori_loop(0, ROWS + 4, coefficients, jnp.zeros((8, LANES), F32))
    for n, shift in enumerate((LANES - 1, 1, LANES - 6, 6)):
        e_coef[n] = 0.5 * (slab + pltpu.roll(slab, shift, 1))

    for slot, row in ((CHUNKS, 0), (CHUNKS + 1, 14)):
        for peer in group:
            row_copy(peer, 0, row, 2, slot, peer).wait_recv()
    for peer in group:
        extra_copy(peer, 0, peer).wait_recv()

    lane32 = lane_iota(32)
    for n, shift in enumerate((LANES - 12, 32)):
        packed = jnp.zeros((32, LANES), F32)
        for g in range(8):
            moved = pltpu.roll(extra[0, 32 * g : 32 * g + 32, :], (shift + 16 * g) % LANES, 1)
            packed = jnp.where((lane32 >= 16 * g) & (lane32 < 16 * g + 16), moved, packed)
        halo_out[n] = packed

    edge_copies = [
        z_copy(halo_out.at[0], halo_in.at[1], 2, before),
        z_copy(halo_out.at[1], halo_in.at[0], 3, after),
        z_copy(rows_v.at[pl.ds(2, 2)], rows_v.at[pl.ds(ROWS + 2, 2)], 4, before),
        z_copy(rows_v.at[pl.ds(ROWS, 2)], rows_v.at[pl.ds(0, 2)], 5, after),
    ]
    for copy in edge_copies:
        copy.start()

    top, bottom = space == 0, space == count - 1

    def put(k, g, column, value):
        high, low = split(value)
        at = pl.ds(pl.multiple_of(k * MODES + g * 16, 16), 16)
        x_hi[at, column : column + LANES] = high
        x_lo[at, column : column + LANES] = low

    column = lax.rem(lane8[:1], 6)
    outside = ((column == 1) & (quarter == 0)) | ((column == 4) & (quarter == 3))

    def extra_terms(g, carry):
        v = extra[0, pl.ds(pl.multiple_of(g * 16, 16), 16), :]
        diffs = [v - pltpu.roll(v, shift, 1) for shift in (LANES - 1, 1, LANES - 6, 6)]
        for k in range(K):
            total = e_coef[0, k : k + 1, :] * diffs[0]
            for n in range(1, 4):
                total = total + e_coef[n, k : k + 1, :] * diffs[n]
            put(k, g, 0, total)
        return carry

    def take_edges():
        for copy in edge_copies:
            copy.wait_recv()

        @pl.when(top)
        def _():
            rows_v[0:2] = jnp.zeros((2, MODES, LANES), F32)

        @pl.when(bottom)
        def _():
            rows_v[ROWS + 2 : ROWS + 4] = jnp.zeros((2, MODES, LANES), F32)

        upper = jnp.where(top, 0.0, halo_in[0])
        lower = jnp.where(bottom, 0.0, halo_in[1])
        for g in range(8):
            at = slice(32 * g, 32 * g + 32)
            value = jnp.where(lane32 < 12, pltpu.roll(upper, (LANES - 16 * g) % LANES, 1), extra[0, at, :])
            inside = (lane32 >= 108) & (lane32 < 120)
            extra[0, at, :] = jnp.where(inside, pltpu.roll(lower, (108 - 16 * g) % LANES, 1), value)

    lane16 = lane_iota(16)

    def terms(base, side_index, index):
        for g in range(GROUPS):
            at = slice(g * 16, g * 16 + 16)
            v = [rows_v[base + n, at, :] for n in range(4)]
            side = extra[side_index, at, :]
            down = [v[n] - v[n + 1] for n in range(3)]
            diffs = []
            for n in range(2):
                here = v[n + 1]
                lane = 6 * (index + n)
                left = jnp.where(lane16 == 0, pltpu.roll(side, LANES - 1 - lane, 1), pltpu.roll(here, 1, 1))
                right = jnp.where(
                    lane16 == LANES - 1, pltpu.roll(side, LANES - 5 - lane, 1), pltpu.roll(here, LANES - 1, 1)
                )
                diffs.append((here - left, here - right))
            for k in range(K):
                flux = [c_down[index - 1 + n, k : k + 1, :] * down[n] for n in range(3)]
                for n in range(2):
                    total = (
                        c_left[index + n, k : k + 1, :] * diffs[n][0]
                        + c_right[index + n, k : k + 1, :] * diffs[n][1]
                    )
                    put(k, g, n * LANES, total + (flux[n + 1] - flux[n]))

    def home_copy(peer, owner_of_block, pair, their_quarter):
        return pltpu.make_async_remote_copy(
            src_ref=rows_v.at[pl.ds(DAMPED + 2 * pair, 2), pl.ds(pl.multiple_of(owner_of_block * BLOCK, BLOCK), BLOCK)],
            dst_ref=home.at[their_quarter, pl.ds(2 * pair, 2)],
            send_sem=out_send.at[pair, peer],
            recv_sem=out_recv.at[pair, their_quarter],
            device_id=(space, peer),
            device_id_type=MESH,
        )

    last = ROWS // 2

    def own_copy(pair):
        return pltpu.make_async_copy(
            rows_v.at[pl.ds(DAMPED + 2 * pair, 2), pl.ds(mine, BLOCK)], home.at[quarter, pl.ds(2 * pair, 2)], own_sem.at[pair]
        )

    again = 2 * last - 2

    def task(n, carry):
        is_extra = (n == 0) | (n == again)
        m = n - jnp.where(n > again, 1, 0)
        is_first = (m == 1) | (lax.rem(m, 2) == 0)
        f = lax.rem(jnp.where(m == 1, 1, m // 2 + 1), last + 1)
        d = lax.rem(jnp.maximum(m - 1, 0) // 2, last)
        base = jnp.where(is_first, 2 * f, FIRST + 2 * d)
        target = jnp.where(is_first, FIRST + 2 * f, DAMPED + 2 * d)
        target = jnp.where(is_extra, DAMPED + ROWS, target)
        index = jnp.where(is_first, 2 * f + 1, 2 * d + 2)

        @pl.when(jnp.logical_not(is_extra) & is_first & (f >= 1) & (f <= CHUNKS))
        def _():
            for peer in group:
                row_copy(peer, 0, 2 * f, 2, f - 1, peer).wait_recv()

        @pl.when(n == again)
        def _():
            take_edges()

        @pl.when(is_extra)
        def _():
            lax.fori_loop(0, GROUPS, extra_terms, 0)

        @pl.when(jnp.logical_not(is_extra))
        def _():
            terms(base, jnp.where(is_first, 0, 1), index)

        result = (
            jnp.dot(mix_hi[...], x_hi[...], preferred_element_type=F32)
            + jnp.dot(mix_hi[...], x_lo[...], preferred_element_type=F32)
            + jnp.dot(mix_lo[...], x_hi[...], preferred_element_type=F32)
        )
        rows_v[target] = jnp.where(is_first & (f == 0) & top, 0.0, result[:, :LANES])
        rows_v[target + 1] = jnp.where(is_first & (f == last) & bottom, 0.0, result[:, LANES:])

        @pl.when(is_extra)
        def _():
            extra[1] = jnp.where(outside, 0.0, rows_v[DAMPED + ROWS])

        @pl.when(jnp.logical_not(is_extra | is_first))
        def _():
            for peer in group:
                home_copy(peer, peer, d, quarter).start()
            own_copy(d).start()

        return carry

    lax.fori_loop(0, 2 * last + 3, task, 0)

    for pair in range(last):
        for peer, peer_quarter in zip(group, group_quarter):
            home_copy(peer, mode, pair, peer_quarter).wait_recv()
        own_copy(pair).wait()

    for slot, row in [(c, 2 * c + 2) for c in range(CHUNKS)] + [(CHUNKS, 0), (CHUNKS + 1, 14)]:
        for peer in group:
            row_copy(peer, 0, row, 2, slot, mode).wait_send()
    for peer in group:
        extra_copy(peer, 0, mode).wait_send()
        for pair in range(ROWS // 2):
            home_copy(peer, peer, pair, quarter).wait_send()
    for copy in gap_copies + edge_copies:
        copy.wait_send()


def arrange(home, out, taken, laid, load_sem, store_sem):
    rows = ROWS // 2
    places = [(n, t) for n in range(2) for t in range(4)]
    stores = [
        pltpu.make_async_copy(laid.at[n, t], out.at[:, n, :, t * LANES : (t + 1) * LANES], store_sem.at[n, t])
        for n, t in places
    ]
    loads = [
        pltpu.make_async_copy(home.at[t, pl.ds(n * rows, rows)], taken.at[n, t], load_sem.at[n, t]) for n, t in places
    ]
    for load in loads:
        load.start()
    for load, store, (n, t) in zip(loads, stores, places):
        load.wait()
        flat = laid.at[n, t].reshape(BLOCK * rows, LANES)
        for r in range(rows):
            flat[pl.ds(r, BLOCK, stride=rows), :] = taken[n, t, r]
        store.start()
    for store in stores:
        store.wait()


def per_device(pressure, gap_terms, coupling, pattern):
    cells = pressure.shape[2]
    vmem = pltpu.VMEM
    result = pl.pallas_call(
        kernel,
        out_shape=jax.ShapeDtypeStruct((4, ROWS, BLOCK, LANES), F32),
        in_specs=[
            pl.BlockSpec(memory_space=pl.ANY),
            pl.BlockSpec(memory_space=pl.ANY),
            pl.BlockSpec(memory_space=pl.ANY),
            pl.BlockSpec(memory_space=pl.ANY),
        ],
        out_specs=pl.BlockSpec(memory_space=pl.ANY),
        scratch_shapes=[
            vmem((4, BLOCK * ROWS, LANES), F32),
            vmem((4, K * ROWS, LANES), F32),
            vmem((K, MODES, MODES), F32),
            vmem((4, 4, K), jnp.int32),
            vmem((DAMPED + ROWS + 2, MODES, LANES), F32),
            vmem((2, MODES, LANES), F32),
            vmem((4, BLOCK, LANES), F32),
            vmem((4, ROWS, BLOCK, LANES), F32),
            vmem((ROWS + 4, K, cells + 2 * LANES), F32),
            vmem((ROWS + 4, K, LANES), F32),
            vmem((ROWS + 4, K, LANES), F32),
            vmem((ROWS + 4, K, LANES), F32),
            vmem((4, K, LANES), F32),
            vmem((MODES, K * MODES), BF16),
            vmem((MODES, K * MODES), BF16),
            vmem((K * MODES, 2 * LANES), BF16),
            vmem((K * MODES, 2 * LANES), BF16),
            vmem((2, 32, LANES), F32),
            vmem((2, 32, LANES), F32),
            pltpu.SemaphoreType.DMA((10,)),
            pltpu.SemaphoreType.DMA((CHUNKS + 3, 4)),
            pltpu.SemaphoreType.DMA((CHUNKS + 3, 4)),
            pltpu.SemaphoreType.DMA((6,)),
            pltpu.SemaphoreType.DMA((6,)),
            pltpu.SemaphoreType.DMA((ROWS // 2, 4)),
            pltpu.SemaphoreType.DMA((ROWS // 2, 4)),
            pltpu.SemaphoreType.DMA((ROWS // 2,)),
        ],
        compiler_params=pltpu.CompilerParams(
            collective_id=0, has_side_effects=True, vmem_limit_bytes=56 * 1024 * 1024
        ),
        cost_estimate=pl.CostEstimate(flops=26_000_000_000, bytes_accessed=7_000_000, transcendentals=0),
        name="galerkin_twice",
    )(pressure.reshape(BLOCK * ROWS, cells), gap_terms.reshape(K * ROWS, cells), coupling, pattern.transpose(1, 2, 0))
    out = pl.pallas_call(
        arrange,
        out_shape=jax.ShapeDtypeStruct((BLOCK, 2, ROWS // 2, cells), F32),
        in_specs=[pl.BlockSpec(memory_space=pl.ANY)],
        out_specs=pl.BlockSpec(memory_space=pl.ANY),
        scratch_shapes=[
            vmem((2, 4, ROWS // 2, BLOCK, LANES), F32),
            vmem((2, 4, BLOCK, ROWS // 2, LANES), F32),
            pltpu.SemaphoreType.DMA((2, 4)),
            pltpu.SemaphoreType.DMA((2, 4)),
        ],
        compiler_params=pltpu.CompilerParams(vmem_limit_bytes=60 * 1024 * 1024),
        cost_estimate=pl.CostEstimate(flops=0, bytes_accessed=4_200_000, transcendentals=0),
        name="arrange",
    )(result)
    return out.reshape(pressure.shape)


def solution(mesh):
    placed = (P("modes", "space", None), P(None, "space", None), P(), P())
    return jax.shard_map(
        per_device, mesh=mesh, in_specs=placed, out_specs=P("modes", "space", None), check_vma=False
    )
```

time: 98.7 us -> 73.9 us (0.75)
  Pallas kernels: 93.8 us -> 73.8 us
  local copies, waits for them, and re-layouts: 4.61 us -> 0 us
    pallas_call x1 -> x2, Pallas kernels: 93.8 us -> 73.8 us  [the longest x1 71.4 us: per_device(): pl.pallas_call(kernel, out_shape=jax.ShapeDtypeStruct((4, ROWS, BLOCK, LA...]
    unnamed x2 -> x0, local copies, waits for them, and re-layouts: 4.61 us -> none
where the time goes in v1:
time: 73.9 us; the launch traced here: 73.8 us
  Pallas kernels  73.8 us (100%)
    pallas_call x1, Pallas kernels, per_device(): pl.pallas_call(kernel, out_shape=jax.ShapeDtypeStruct((4, ROWS, BLOCK, LA...  71.4 us
    pallas_call x1, Pallas kernels, per_device(): pl.pallas_call(arrange, out_shape=jax.ShapeDtypeStruct((BLOCK, 2, ROWS //...  2.46 us

profile of v1, /device:TPU:1, one launch (start us, length us, event | category | flops | bytes accessed | tf_op | source)
XLA Modules:
  0.0 73.8 jit_solution(3050385132886136605)
XLA Ops:
  0.0 71.4 %galerkin_twice.1.home = f32[4,16,64,128]{3,2,1,0:T(8,128)} custom-call(f32[1024,512]{1,0:T(8,128)} %bitcast.4, f32[128,512]{1,0:T(8,128)} %bitcast.5, f32[8,256,256]{2,1,0:T(8,128)} %coupling.1, s32[4,4,8]{2,1,0:T(4,128)} %bitcast.6), custom_call_target="tpu_custom_call" | custom-call | flops 25999998976 | bytes 7000000 | tf_op jit(solution)/shard_map/galerkin_twice/pallas_call | solution.py:405
  71.4 2.5 %arrange.1 = f32[64,2,8,512]{3,2,1,0:T(8,128)} custom-call(f32[4,16,64,128]{3,2,1,0:T(8,128)} %galerkin_twice.1.home), custom_call_target="tpu_custom_call" | custom-call | bytes 4200000 | tf_op jit(solution)/shard_map/arrange/pallas_call | solution.py:450

commit v2 on v1

--- a/solution.py
+++ b/solution.py
@@ -1,3 +1,5 @@
+import functools
+
 import jax
 import jax.numpy as jnp
 from jax import lax
@@ -14,6 +16,8 @@
 ZRUN = 8
 GROUPS = MODES // 16
 CHUNKS = 6
+GATE = 3
+MEET = 1
 FIRST = ROWS + 4
 DAMPED = 2 * ROWS + 6
 F32 = jnp.float32
@@ -32,8 +36,8 @@
 def kernel(
     press, gap, coupling, pattern, home,
     strip, gap_in, coup, pattern_in, rows_v, extra, extra_own, sendrows,
-    gap_pad, c_right, c_left, c_down, e_coef, mix_hi, mix_lo, x_hi, x_lo, halo_out, halo_in,
-    load_sem, in_send, in_recv, z_send, z_recv, out_send, out_recv, own_sem,
+    gap_pad, c_right, c_left, c_down, e_coef, mix_hi, mix_lo, x_hi, x_lo, halo_out, halo_in, gap_halo, gap_extra,
+    load_sem, in_send, in_recv, z_send, z_recv, out_send, out_recv, own_sem, entered, beside_in, proceed,
 ):
     space = lax.axis_index("space")
     mode = lax.axis_index("modes")
@@ -65,11 +69,18 @@
     for load in press_loads + gap_loads + [coup_load, pattern_load]:
         load.start()
 
+    is_gate = mode == GATE
     barrier = pltpu.get_barrier_semaphore()
     for peer in group:
-        pl.semaphore_signal(barrier, inc=1, device_id=(space, peer), device_id_type=MESH)
-    for peer in (before, after):
-        pl.semaphore_signal(barrier, inc=1, device_id=peer, device_id_type=MESH)
+
+        @pl.when(peer != GATE)
+        def _():
+            pl.semaphore_signal(barrier, inc=1, device_id=(space, peer), device_id_type=MESH)
+
+    @pl.when(is_gate)
+    def _():
+        for peer in (before, after):
+            pl.semaphore_signal(barrier, inc=1, device_id=peer, device_id_type=MESH)
 
     for load in press_loads:
         load.wait()
@@ -96,7 +107,24 @@
 
     lax.fori_loop(0, BLOCK // 8, own_rows, 0)
 
-    pl.semaphore_wait(barrier, 5)
+    @pl.when(jnp.logical_not(is_gate))
+    def _():
+        pl.semaphore_wait(barrier, 3)
+        pl.semaphore_signal(entered, inc=1, device_id=(space, GATE), device_id_type=MESH)
+
+    @pl.when(is_gate)
+    def _():
+        pl.semaphore_wait(entered, 3)
+
+    def meet_neighbours():
+        pl.semaphore_wait(barrier, 2)
+        for peer in (before, after):
+            pl.semaphore_signal(beside_in, inc=1, device_id=peer, device_id_type=MESH)
+
+    def pass_on():
+        pl.semaphore_wait(beside_in, 2)
+        for peer in group:
+            pl.semaphore_signal(proceed, inc=1, device_id=(space, peer), device_id_type=MESH)
 
     mine = pl.multiple_of(mode * BLOCK, BLOCK)
 
@@ -120,14 +148,12 @@
             device_id_type=MESH,
         )
 
-    for row, slot in ((0, CHUNKS), (14, CHUNKS + 1)):
+    for peer, peer_quarter in zip(group, group_quarter):
+        extra_copy(peer, peer_quarter, mode).start()
+    for row in (0, 2, 14, 4, 6, 8, 10, 12):
+        slot = {0: CHUNKS, 14: CHUNKS + 1}.get(row, row // 2 - 1)
         for peer, peer_quarter in zip(group, group_quarter):
             row_copy(peer, peer_quarter, row, 2, slot, mode).start()
-    for peer, peer_quarter in zip(group, group_quarter):
-        extra_copy(peer, peer_quarter, mode).start()
-    for c in range(CHUNKS):
-        for peer, peer_quarter in zip(group, group_quarter):
-            row_copy(peer, peer_quarter, 2 * c + 2, 2, c, mode).start()
 
     for load in gap_loads:
         load.wait()
@@ -135,7 +161,8 @@
         slabs = [gap_in[t, pl.ds(r, K, stride=ROWS), :] for t in range(4)]
         slabs = [jnp.broadcast_to(slabs[0][:, :1], (K, LANES)), *slabs, jnp.broadcast_to(slabs[3][:, LANES - 1 :], (K, LANES))]
         for t in range(6):
-            gap_pad[r + 2, :, columns(t)] = slabs[t]
+            for place in {0: (0, 1, 2), ROWS - 1: (ROWS + 1, ROWS + 2, ROWS + 3)}.get(r, (r + 2,)):
+                gap_pad[place, :, columns(t)] = slabs[t]
 
     def z_copy(source, target, slot, device):
         return pltpu.make_async_remote_copy(
@@ -144,11 +171,9 @@
         )
 
     gap_copies = [
-        z_copy(gap_pad.at[pl.ds(2, 2)], gap_pad.at[pl.ds(ROWS + 2, 2)], 0, before),
-        z_copy(gap_pad.at[pl.ds(ROWS, 2)], gap_pad.at[pl.ds(0, 2)], 1, after),
+        z_copy(gap_pad.at[pl.ds(2, 2)], gap_halo.at[1], 0, before),
+        z_copy(gap_pad.at[pl.ds(ROWS, 2)], gap_halo.at[0], 1, after),
     ]
-    for copy in gap_copies:
-        copy.start()
 
     extra[0, pl.ds(mine, BLOCK), :] = extra_own[quarter]
     for r in range(ROWS):
@@ -169,23 +194,13 @@
             mix_hi[b * BLOCK : (b + 1) * BLOCK, k * MODES : (k + 1) * MODES] = high
             mix_lo[b * BLOCK : (b + 1) * BLOCK, k * MODES : (k + 1) * MODES] = low
 
-    for copy in gap_copies:
-        copy.wait_recv()
-
-    @pl.when(space == 0)
-    def _():
-        gap_pad[1] = gap_pad[2]
-
-    @pl.when(space == count - 1)
-    def _():
-        gap_pad[ROWS + 2] = gap_pad[ROWS + 1]
-
     def tile(index, side):
         return gap_pad[index, :, pl.ds(pl.multiple_of((quarter + side) * LANES, LANES), LANES)]
 
     lane8 = lane_iota(8)
 
-    def coefficients(index, slab):
+    def coefficients(step, carry, skip):
+        index = step + jnp.where(step >= 2, skip, 0)
         left, here, right = tile(index, 0), tile(index, 1), tile(index, 2)
         below = tile(jnp.minimum(index + 1, ROWS + 3), 1)
         next_cell = jnp.where(lane8 == LANES - 1, pltpu.roll(right, LANES - 1, 1), pltpu.roll(here, LANES - 1, 1))
@@ -196,17 +211,22 @@
         edge_right = jnp.where(lane8 < 2, pltpu.roll(here, 2, 1), pltpu.roll(right, 2, 1))
         both = jnp.where(lane8 < 3, edge_left, pltpu.roll(edge_right, 2, 1))
         start = 6 * index
-        return jnp.where((lane8 >= start) & (lane8 < start + 6), pltpu.roll(both, start, 1), slab)
-
-    slab = lax.fori_loop(0, ROWS + 4, coefficients, jnp.zeros((8, LANES), F32))
-    for n, shift in enumerate((LANES - 1, 1, LANES - 6, 6)):
-        e_coef[n] = 0.5 * (slab + pltpu.roll(slab, shift, 1))
-
-    for slot, row in ((CHUNKS, 0), (CHUNKS + 1, 14)):
-        for peer in group:
-            row_copy(peer, 0, row, 2, slot, peer).wait_recv()
+        inside = (lane8 >= start) & (lane8 < start + 6)
+        gap_extra[...] = jnp.where(inside, pltpu.roll(both, start, 1), gap_extra[...])
+        return carry
+
+    def tables(steps, skip):
+        lax.fori_loop(0, steps, functools.partial(coefficients, skip=skip), 0)
+        slab = gap_extra[...]
+        for n, shift in enumerate((LANES - 1, 1, LANES - 6, 6)):
+            e_coef[n] = 0.5 * (slab + pltpu.roll(slab, shift, 1))
+
+    gap_extra[...] = jnp.zeros((K, LANES), F32)
+    tables(ROWS + 4, 0)
+
     for peer in group:
         extra_copy(peer, 0, peer).wait_recv()
+        row_copy(peer, 0, 0, 2, CHUNKS, peer).wait_recv()
 
     lane32 = lane_iota(32)
     for n, shift in enumerate((LANES - 12, 32)):
@@ -222,8 +242,12 @@
         z_copy(rows_v.at[pl.ds(2, 2)], rows_v.at[pl.ds(ROWS + 2, 2)], 4, before),
         z_copy(rows_v.at[pl.ds(ROWS, 2)], rows_v.at[pl.ds(0, 2)], 5, after),
     ]
-    for copy in edge_copies:
-        copy.start()
+
+    def send_edges():
+        for peer in group:
+            row_copy(peer, 0, 14, 2, CHUNKS + 1, peer).wait_recv()
+        for copy in gap_copies + edge_copies:
+            copy.start()
 
     top, bottom = space == 0, space == count - 1
 
@@ -247,8 +271,18 @@
         return carry
 
     def take_edges():
-        for copy in edge_copies:
+        for copy in gap_copies + edge_copies:
             copy.wait_recv()
+
+        @pl.when(jnp.logical_not(top))
+        def _():
+            gap_pad[0:2] = gap_halo[0]
+
+        @pl.when(jnp.logical_not(bottom))
+        def _():
+            gap_pad[ROWS + 2 : ROWS + 4] = gap_halo[1]
+
+        tables(5, ROWS - 1)
 
         @pl.when(top)
         def _():
@@ -326,6 +360,22 @@
         def _():
             for peer in group:
                 row_copy(peer, 0, 2 * f, 2, f - 1, peer).wait_recv()
+
+        @pl.when((n == MEET) & is_gate)
+        def _():
+            meet_neighbours()
+
+        @pl.when((n == MEET + 1) & is_gate)
+        def _():
+            pass_on()
+
+        @pl.when((n == MEET + 2) & jnp.logical_not(is_gate))
+        def _():
+            pl.semaphore_wait(proceed, 1)
+
+        @pl.when(n == MEET + 2)
+        def _():
+            send_edges()
 
         @pl.when(n == again)
         def _():
@@ -432,6 +482,8 @@
             vmem((K * MODES, 2 * LANES), BF16),
             vmem((2, 32, LANES), F32),
             vmem((2, 32, LANES), F32),
+            vmem((2, 2, K, cells + 2 * LANES), F32),
+            vmem((K, LANES), F32),
             pltpu.SemaphoreType.DMA((10,)),
             pltpu.SemaphoreType.DMA((CHUNKS + 3, 4)),
             pltpu.SemaphoreType.DMA((CHUNKS + 3, 4)),
@@ -440,6 +492,9 @@
             pltpu.SemaphoreType.DMA((ROWS // 2, 4)),
             pltpu.SemaphoreType.DMA((ROWS // 2, 4)),
             pltpu.SemaphoreType.DMA((ROWS // 2,)),
+            pltpu.SemaphoreType.REGULAR,
+            pltpu.SemaphoreType.REGULAR,
+            pltpu.SemaphoreType.REGULAR,
         ],
         compiler_params=pltpu.CompilerParams(
             collective_id=0, has_side_effects=True, vmem_limit_bytes=56 * 1024 * 1024

time: 73.9 us -> 68.8 us (0.931)
  Pallas kernels: 73.8 us -> 68.7 us
    pallas_call x1, Pallas kernels: 71.4 us -> 66.2 us  [per_device(): pl.pallas_call(kernel, out_shape=jax.ShapeDtypeStruct((4, ROWS, BLOCK, LA...]
where the time goes in v2:
time: 68.8 us; the launch traced here: 68.7 us
  Pallas kernels  68.7 us (100%)
    pallas_call x1, Pallas kernels, per_device(): pl.pallas_call(kernel, out_shape=jax.ShapeDtypeStruct((4, ROWS, BLOCK, LA...  66.2 us
    pallas_call x1, Pallas kernels, per_device(): pl.pallas_call(arrange, out_shape=jax.ShapeDtypeStruct((BLOCK, 2, ROWS //...  2.46 us

profile of v2, /device:TPU:1, one launch (start us, length us, event | category | flops | bytes accessed | tf_op | source)
XLA Modules:
  0.0 68.7 jit_solution(14792697135628028627)
XLA Ops:
  0.0 66.2 %galerkin_twice.1.home = f32[4,16,64,128]{3,2,1,0:T(8,128)} custom-call(f32[1024,512]{1,0:T(8,128)} %bitcast.4, f32[128,512]{1,0:T(8,128)} %bitcast.5, f32[8,256,256]{2,1,0:T(8,128)} %coupling.1, s32[4,4,8]{2,1,0:T(4,128)} %bitcast.6), custom_call_target="tpu_custom_call" | custom-call | flops 25999998976 | bytes 7000000 | tf_op jit(solution)/shard_map/galerkin_twice/pallas_call | solution.py:455
  66.2 2.5 %arrange.1 = f32[64,2,8,512]{3,2,1,0:T(8,128)} custom-call(f32[4,16,64,128]{3,2,1,0:T(8,128)} %galerkin_twice.1.home), custom_call_target="tpu_custom_call" | custom-call | bytes 4200000 | tf_op jit(solution)/shard_map/arrange/pallas_call | solution.py:505

commit v3 on v2

--- a/solution.py
+++ b/solution.py
@@ -383,7 +383,7 @@
 
         @pl.when(is_extra)
         def _():
-            lax.fori_loop(0, GROUPS, extra_terms, 0)
+            lax.fori_loop(0, GROUPS, extra_terms, 0, unroll=8)
 
         @pl.when(jnp.logical_not(is_extra))
         def _():

time: 68.8 us -> 67.7 us (0.984)
  Pallas kernels: 68.7 us -> 67.6 us
    pallas_call x1, Pallas kernels: 66.2 us -> 65.2 us  [per_device(): pl.pallas_call(kernel, out_shape=jax.ShapeDtypeStruct((4, ROWS, BLOCK, LA...]
where the time goes in v3:
time: 67.7 us; the launch traced here: 67.6 us
  Pallas kernels  67.6 us (100%)
    pallas_call x1, Pallas kernels, per_device(): pl.pallas_call(kernel, out_shape=jax.ShapeDtypeStruct((4, ROWS, BLOCK, LA...  65.2 us
    pallas_call x1, Pallas kernels, per_device(): pl.pallas_call(arrange, out_shape=jax.ShapeDtypeStruct((BLOCK, 2, ROWS //...  2.46 us

profile of v3, /device:TPU:1, one launch (start us, length us, event | category | flops | bytes accessed | tf_op | source)
XLA Modules:
  0.0 67.6 jit_solution(17879177461118673967)
XLA Ops:
  0.0 65.2 %galerkin_twice.1.home = f32[4,16,64,128]{3,2,1,0:T(8,128)} custom-call(f32[1024,512]{1,0:T(8,128)} %bitcast.4, f32[128,512]{1,0:T(8,128)} %bitcast.5, f32[8,256,256]{2,1,0:T(8,128)} %coupling.1, s32[4,4,8]{2,1,0:T(4,128)} %bitcast.6), custom_call_target="tpu_custom_call" | custom-call | flops 25999998976 | bytes 7000000 | tf_op jit(solution)/shard_map/galerkin_twice/pallas_call | solution.py:455
  65.2 2.5 %arrange.1 = f32[64,2,8,512]{3,2,1,0:T(8,128)} custom-call(f32[4,16,64,128]{3,2,1,0:T(8,128)} %galerkin_twice.1.home), custom_call_target="tpu_custom_call" | custom-call | bytes 4200000 | tf_op jit(solution)/shard_map/arrange/pallas_call | solution.py:505

commit v4 on v3

--- a/solution.py
+++ b/solution.py
@@ -150,7 +150,7 @@
 
     for peer, peer_quarter in zip(group, group_quarter):
         extra_copy(peer, peer_quarter, mode).start()
-    for row in (0, 2, 14, 4, 6, 8, 10, 12):
+    for row in (0, 14, 2, 4, 6, 8, 10, 12):
         slot = {0: CHUNKS, 14: CHUNKS + 1}.get(row, row // 2 - 1)
         for peer, peer_quarter in zip(group, group_quarter):
             row_copy(peer, peer_quarter, row, 2, slot, mode).start()

time: 67.7 us -> 70.5 us (1.041)
  Pallas kernels: 67.6 us -> 70.4 us
    pallas_call x1, Pallas kernels: 65.2 us -> 68 us  [per_device(): pl.pallas_call(kernel, out_shape=jax.ShapeDtypeStruct((4, ROWS, BLOCK, LA...]
where the time goes in v4:
time: 70.5 us; the launch traced here: 70.4 us
  Pallas kernels  70.4 us (100%)
    pallas_call x1, Pallas kernels, per_device(): pl.pallas_call(kernel, out_shape=jax.ShapeDtypeStruct((4, ROWS, BLOCK, LA...  68 us
    pallas_call x1, Pallas kernels, per_device(): pl.pallas_call(arrange, out_shape=jax.ShapeDtypeStruct((BLOCK, 2, ROWS //...  2.46 us

profile of v4, /device:TPU:1, one launch (start us, length us, event | category | flops | bytes accessed | tf_op | source)
XLA Modules:
  0.0 70.4 jit_solution(5684784844966635306)
XLA Ops:
  0.0 68.0 %galerkin_twice.1.home = f32[4,16,64,128]{3,2,1,0:T(8,128)} custom-call(f32[1024,512]{1,0:T(8,128)} %bitcast.4, f32[128,512]{1,0:T(8,128)} %bitcast.5, f32[8,256,256]{2,1,0:T(8,128)} %coupling.1, s32[4,4,8]{2,1,0:T(4,128)} %bitcast.6), custom_call_target="tpu_custom_call" | custom-call | flops 25999998976 | bytes 7000000 | tf_op jit(solution)/shard_map/galerkin_twice/pallas_call | solution.py:455
  68.0 2.5 %arrange.1 = f32[64,2,8,512]{3,2,1,0:T(8,128)} custom-call(f32[4,16,64,128]{3,2,1,0:T(8,128)} %galerkin_twice.1.home), custom_call_target="tpu_custom_call" | custom-call | bytes 4200000 | tf_op jit(solution)/shard_map/arrange/pallas_call | solution.py:505
